TPU v7x, 256 devices: a whole 4x4x8 slice. The times are simulated.
256 devices in a mesh: group: 32 (over z, y), tensor: 8 (over x, core).
Axes of the slice: x: 4, y: 4, z: 8, core: 2. Of those that a mesh axis runs over, the one named last changes fastest.
Arguments:
- states: bfloat16 [2048, 12, 5120], P('group', None, 'tensor'), may hold values from -6 to 6
- norm_gain: float32 [5120], replicated, may hold values from 0.5 to 1.5
- w_query: bfloat16 [5120, 3072], P(None, 'tensor'), may hold values from -0.078125 to 0.078125
- w_key: bfloat16 [5120, 1024], P(None, 'tensor'), may hold values from -0.078125 to 0.078125
- w_value: bfloat16 [5120, 1024], P(None, 'tensor'), may hold values from -0.078125 to 0.078125
- w_out: bfloat16 [3072, 5120], P('tensor'), may hold values from -0.109375 to 0.109375
- key_cache: bfloat16 [2048, 128, 1024], P('group', None, 'tensor'), may hold values from -64 to 64
- value_cache: bfloat16 [2048, 128, 1024], P('group', None, 'tensor'), may hold values from -6 to 6
- ancestor_group: int32 [2048, 1], replicated, may hold values from 0 to 31; in each aligned block of 64 rows (0 to 63, 64 to 127, ...) at most 4 rows name the same one
- ancestor_slot: int32 [2048], replicated, may hold values from 0 to 63
- lengths: int32 [2048], replicated, may hold values from 16 to 128
Outputs:
- attn_out: bfloat16 [2048, 12, 5120], P('group', None, 'tensor')
Inputs may be any that keep to these rules, and one draw needn't show every extreme that they name: `ancestor_group`: the particles of one group (aligned blocks of 64) name no group more than 4 times.
All inputs are finite; a program needn't handle non-finite values.
Results may differ from a plain program's by a relative error of at most 0.022.
Values may be sent and summed in bfloat16 or wider, within the bound.
A program may use at most 128 MiB of HBM per device.

v0:
```python
import math

import jax
import jax.numpy as jnp
from jax import lax
from jax.sharding import PartitionSpec as P

HEAD = 128


theta_base = 1000000.0
norm_eps = 1e-06


def rope_tables(positions, half_width):
    freq_index = jnp.arange(half_width, dtype=jnp.float32)
    inverse = theta_base ** (-2.0 * freq_index / (2 * half_width))
    angles = positions.astype(jnp.float32)[..., None] * inverse
    return (jnp.cos(angles), jnp.sin(angles))


def rotate(vectors, cos_table, sin_table):
    half_width = cos_table.shape[-1]
    front_half = vectors[..., :half_width]
    back_half = vectors[..., half_width:]
    cos_wide = cos_table[:, :, None, :]
    sin_wide = sin_table[:, :, None, :]
    return jnp.concatenate(
        [
            front_half * cos_wide - back_half * sin_wide,
            back_half * cos_wide + front_half * sin_wide,
        ],
        axis=-1,
    )


def finish_softmax(scores, values, form, item_count, step_count, q_local, head_size):
    peak = jnp.max(scores, axis=-1, keepdims=True)
    weights = jnp.exp(scores - peak).astype(jnp.bfloat16)
    summed = jnp.sum(weights.astype(jnp.float32), axis=-1)
    output = jnp.einsum(form, weights, values, preferred_element_type=jnp.float32)
    return (
        output.reshape(item_count, step_count, q_local, head_size),
        peak[..., 0].reshape(item_count, step_count, q_local),
        summed.reshape(item_count, step_count, q_local),
    )


def cache_attention(queries, keys, values, spans, kv_local):
    item_count, step_count, q_local, head_size = queries.shape
    group_size = q_local // kv_local
    row_count = keys.shape[1]
    grouped = queries.reshape(item_count, step_count, kv_local, group_size, head_size)
    key_heads = keys.reshape(item_count, row_count, kv_local, head_size)
    value_heads = values.reshape(item_count, row_count, kv_local, head_size)
    scores = jnp.einsum(
        "nsvgd,ncvd->nsvgc", grouped, key_heads, preferred_element_type=jnp.float32
    ) * (1.0 / math.sqrt(head_size))
    usable = jnp.arange(row_count, dtype=jnp.int32)[None, :] < spans[:, None]
    scores = jnp.where(usable[:, None, None, None, :], scores, -jnp.inf)
    return finish_softmax(
        scores, value_heads, "nsvgc,ncvd->nsvgd", item_count, step_count, q_local, head_size
    )


def fresh_attention(queries, keys, values, kv_local):
    item_count, step_count, q_local, head_size = queries.shape
    group_size = q_local // kv_local
    grouped = queries.reshape(item_count, step_count, kv_local, group_size, head_size)
    scores = jnp.einsum("nsvgd,ntvd->nsvgt", grouped, keys, preferred_element_type=jnp.float32) * (
        1.0 / math.sqrt(head_size)
    )
    causal = (
        jnp.arange(step_count, dtype=jnp.int32)[None, :]
        <= jnp.arange(step_count, dtype=jnp.int32)[:, None]
    )
    scores = jnp.where(causal[None, :, None, None, :], scores, -jnp.inf)
    return finish_softmax(
        scores, values, "nsvgt,ntvd->nsvgd", item_count, step_count, q_local, head_size
    )


def combine_parts(cache_parts, new_parts):
    cache_out, cache_peak, cache_total = cache_parts
    new_out, new_peak, new_total = new_parts
    peak = jnp.maximum(cache_peak, new_peak)
    cache_scale = jnp.exp(cache_peak - peak)
    new_scale = jnp.exp(new_peak - peak)
    upper = cache_out * cache_scale[..., None] + new_out * new_scale[..., None]
    lower = cache_total * cache_scale + new_total * new_scale
    return (upper / lower[..., None]).astype(jnp.bfloat16)


def local(
    states,
    norm_gain,
    w_query,
    w_key,
    w_value,
    w_out,
    key_cache,
    value_cache,
    ancestor_group,
    ancestor_slot,
    lengths,
):
    part_count = states.shape[0]
    step_count = states.shape[1]
    row_count = key_cache.shape[1]
    cache_width = key_cache.shape[2]
    kv_local = cache_width // HEAD
    q_local = w_query.shape[1] // HEAD
    groups_total = lax.axis_size("group")
    capacity = max(2, (2 * part_count + groups_total - 1) // groups_total)
    my_group = lax.axis_index("group")
    whole = lax.all_gather(states, "tensor", axis=2, tiled=True)
    widened = whole.astype(jnp.float32)
    scale_inv = lax.rsqrt(jnp.mean(widened * widened, axis=-1, keepdims=True) + norm_eps)
    normed = (
        (widened * scale_inv * norm_gain).astype(jnp.bfloat16).reshape(part_count * step_count, -1)
    )
    queries = jnp.dot(normed, w_query, preferred_element_type=jnp.float32).reshape(
        part_count, step_count, q_local, HEAD
    )
    new_keys = jnp.dot(normed, w_key, preferred_element_type=jnp.float32).reshape(
        part_count, step_count, kv_local, HEAD
    )
    new_values = jnp.dot(normed, w_value, preferred_element_type=jnp.float32).reshape(
        part_count, step_count, kv_local, HEAD
    )
    sources = ancestor_group[:, 0]
    ancestors = sources * part_count + ancestor_slot
    my_ancestors = lax.dynamic_slice_in_dim(ancestors, my_group * part_count, part_count)
    my_spans = jnp.take(lengths, my_ancestors)
    positions = my_spans[:, None] + jnp.arange(step_count, dtype=jnp.int32)[None, :]
    cos_table, sin_table = rope_tables(positions, HEAD // 2)
    q_rot = rotate(queries, cos_table, sin_table).astype(jnp.bfloat16)
    k_rot = rotate(new_keys, cos_table, sin_table).astype(jnp.bfloat16)
    v_new = new_values.astype(jnp.bfloat16)
    block_sources = sources.reshape(groups_total, part_count)
    block_slots = ancestor_slot.reshape(groups_total, part_count)
    matching = block_sources[:, :, None] == block_sources[:, None, :]
    earlier = jnp.arange(part_count)[None, :] < jnp.arange(part_count)[:, None]
    block_rank = jnp.sum(matching & earlier[None], axis=2)
    my_sources = lax.dynamic_index_in_dim(block_sources, my_group, 0, keepdims=False)
    my_rank = lax.dynamic_index_in_dim(block_rank, my_group, 0, keepdims=False)
    flat_slot = my_sources * capacity + my_rank
    chosen = (block_sources[:, None, :] == my_group) & (
        block_rank[:, None, :] == jnp.arange(capacity, dtype=jnp.int32)[None, :, None]
    )
    local_index = jnp.sum(jnp.where(chosen, block_slots[:, None, :], 0), axis=2).reshape(-1)
    sent_keys = jnp.take(key_cache, local_index, axis=0).reshape(
        groups_total, capacity, row_count, cache_width
    )
    sent_values = jnp.take(value_cache, local_index, axis=0).reshape(
        groups_total, capacity, row_count, cache_width
    )
    arrived_keys, arrived_values = (
        lax.all_to_all(sent_keys, "group", split_axis=0, concat_axis=0, tiled=True),
        lax.all_to_all(sent_values, "group", split_axis=0, concat_axis=0, tiled=True),
    )
    own_keys = jnp.take(
        arrived_keys.reshape(groups_total * capacity, row_count, cache_width), flat_slot, axis=0
    )
    own_values = jnp.take(
        arrived_values.reshape(groups_total * capacity, row_count, cache_width), flat_slot, axis=0
    )
    cache_parts = cache_attention(q_rot, own_keys, own_values, my_spans, kv_local)
    new_parts = fresh_attention(q_rot, k_rot, v_new, kv_local)
    attended = combine_parts(cache_parts, new_parts).reshape(
        part_count * step_count, q_local * HEAD
    )
    partial_value = jnp.dot(attended, w_out, preferred_element_type=jnp.float32).reshape(
        part_count, step_count, -1
    )
    return lax.psum_scatter(
        partial_value.astype(jnp.bfloat16), "tensor", scatter_dimension=2, tiled=True
    )


def solution(mesh):
    in_specs = (
        P("group", None, "tensor"),
        P(),
        P(None, "tensor"),
        P(None, "tensor"),
        P(None, "tensor"),
        P("tensor", None),
        P("group", None, "tensor"),
        P("group", None, "tensor"),
        P(),
        P(),
        P(),
    )
    out_specs = P("group", None, "tensor")
    return jax.shard_map(local, mesh=mesh, in_specs=in_specs, out_specs=out_specs, check_vma=False)
```

profile of v0, /device:TPU:1, one launch (start us, length us, event | category | flops | bytes accessed | tf_op | source)
XLA Modules:
  0.0 420.6 jit_solution(15627293491454840048)
XLA Ops:
  10.7 3.0 gather_fusion.3
  13.7 4.7 %gather_fusion.1 = bf16[128,128,128]{2,1,0:T(8,128)(2,1)} fusion(bf16[64,128,128]{2,1,0:T(8,128)(2,1)} %param.22, s32[1024]{0:T(1024)S(1)} %pad_clamp_fusion.2), kind=kCustom, calls=%fused_computation.clone | custom fusion | bytes 8389120 | tf_op jit(solution)/shard_map/jit(_take)/gather | solution.py:155
  18.4 6.0 %broadcast_select_fusion.1 = (bf16[128,128,128]{2,1,0:T(8,128)(2,1)}, bf16[128,128,128]{2,1,0:T(8,128)(2,1)}) fusion(bf16[128,128,128]{2,1,0:T(8,128)(2,1)} %gather_fusion.1, pred[128]{0:T(512)(128)(4,1)S(1)} %compare_and_fusion.1, bf16[128,128,128]{2,1,0:T(8,128)(2,1)} %gather_fusion.3), kind=kLoop, calls=%fused_computation.14 | loop fusion | flops 4194304 | bytes 16777344 | tf_op jit(solution)/shard_map/jit(_take)/select_n | solution.py:155
  24.4 12.2 %all-to-all-start.1 = ((bf16[32,4,128,128]{3,2,1,0:T(8,128)(2,1)}), bf16[32,4,128,128]{3,2,1,0:T(8,128)(2,1)}, u32[]{:S(2)}, u32[]{:S(2)}) async-start(bf16[32,4,128,128]{3,2,1,0:T(8,128)(2,1)} %bitcast.108), calls=%async_computation.1 | async-start | bytes 8388608 | tf_op jit(solution)/shard_map/all_to_all | solution.py:159
  37.4 92.3 %all-to-all-done.1 = bf16[32,4,128,128]{3,2,1,0:T(8,128)(2,1)} async-done(((bf16[32,4,128,128]{3,2,1,0:T(8,128)(2,1)}), bf16[32,4,128,128]{3,2,1,0:T(8,128)(2,1)}, u32[]{:S(2)}, u32[]{:S(2)}) %all-to-all-start.1) | async-done | bytes 4194336 | tf_op jit(solution)/shard_map/all_to_all | solution.py:159
  129.7 8.4 %all-to-all-start = ((bf16[32,4,128,128]{3,2,1,0:T(8,128)(2,1)}), bf16[32,4,128,128]{3,2,1,0:T(8,128)(2,1)}, u32[]{:S(2)}, u32[]{:S(2)}) async-start(bf16[32,4,128,128]{3,2,1,0:T(8,128)(2,1)} %bitcast.107), calls=%async_computation | async-start | bytes 8388608 | tf_op jit(solution)/shard_map/all_to_all | solution.py:160
  138.1 6.2 %copy.68 = bf16[5120,384]{0,1:T(8,128)(2,1)} copy(bf16[5120,384]{1,0:T(8,128)(2,1)} %param.17) | data formatting | bytes 7864320 | tf_op args[2]
  147.5 4.4 %gather_fusion.4 = bf16[64,128,128]{2,1,0:T(8,128)(2,1)} fusion(bf16[128,128,128]{2,1,0:T(8,128)(2,1)} %bitcast.7, s32[1024]{0:T(1024)S(1)} %pad_clamp_fusion.1), kind=kCustom, calls=%fused_computation.3.clone | custom fusion | bytes 4194560 | tf_op jit(solution)/shard_map/jit(_take)/gather | solution.py:162
  151.9 79.4 %all-to-all-done = bf16[32,4,128,128]{3,2,1,0:T(8,128)(2,1)} async-done(((bf16[32,4,128,128]{3,2,1,0:T(8,128)(2,1)}), bf16[32,4,128,128]{3,2,1,0:T(8,128)(2,1)}, u32[]{:S(2)}, u32[]{:S(2)}) %all-to-all-start) | async-done | bytes 4194336 | tf_op jit(solution)/shard_map/all_to_all | solution.py:160
  231.3 4.4 %gather_fusion.2 = bf16[64,128,128]{2,1,0:T(8,128)(2,1)} fusion(bf16[128,128,128]{2,1,0:T(8,128)(2,1)} %bitcast.2, s32[1024]{0:T(1024)S(1)} %pad_clamp_fusion.1), kind=kCustom, calls=%fused_computation.1.clone | custom fusion | bytes 4194560 | tf_op jit(solution)/shard_map/jit(_take)/gather | solution.py:165
  235.8 5.0 %fusion = f32[64,12]{0,1:T(8,128)S(1)} fusion(bf16[64,12,5120]{2,0,1:T(8,128)(2,1)} %all-gather.2.cloned.1.call-done), kind=kLoop, calls=%fused_computation.7 | loop fusion | flops 11795712 | bytes 7867392 | tf_op jit(solution)/shard_map/reduce_sum | solution.py:118
  241.2 3.8 fusion.28
  245.0 2.0 fusion.60
  247.1 4.4 %fusion.3 = f32[64,12,3,128]{3,0,2,1:T(8,128)S(1)} fusion(bf16[3,128,5120,1]{2,1,0,3:T(8,128)(2,1)S(1)} %bitcast.110, bf16[64,12,5120]{2,0,1:T(8,128)(2,1)S(1)} %copy-done.3, f32[5120]{0:T(1024)S(1)} %copy-done.11, f32[64,12]{0,1:T(8,128)S(1)} %add_rsqrt_fusion), kind=kOutput, calls=%fused_computation.11 | convolution fusion | flops 3035627520 | bytes 12999680 | tf_op jit(solution)/shard_map/dot_general | solution.py:122
  253.2 1.6 fusion.70
  256.0 5.5 %fusion.38 = bf16[64,12,128,1]{2,0,1,3:T(8,128)(2,1)S(1)} fusion(bf16[5120,128]{1,0:T(8,128)(2,1)S(1)} %copy-done.10, bf16[64,12,5120]{2,0,1:T(8,128)(2,1)} %all-gather.2.cloned.1.call-done, f32[5120]{0:T(1024)S(1)} %copy-done.11, f32[64,12]{0,1:T(8,128)S(1)} %add_rsqrt_fusion), kind=kOutput, calls=%fused_computation.44 | convolution fusion | flops 1022459904 | bytes 9395200 | tf_op jit(solution)/shard_map/dot_general | solution.py:128
  261.5 1.7 convolution_bitcast_fusion
  263.8 2.0 copy.79
  266.8 4.7 %bitcast_reduce_fusion = (f32[64,12,3]{1,2,0:T(4,128)S(1)}, f32[64,1,128,12,3]{2,3,4,0,1:T(8,128)}) fusion(bf16[64,12,3,128]{3,0,2,1:T(8,128)(2,1)} %copy-done.5, bf16[64,128,128]{2,1,0:T(8,128)(2,1)} %gather_fusion.4, pred[64]{0:T(512)(128)(4,1)S(1)} %get-tuple-element.10, pred[64,128]{1,0:T(8,128)(4,1)S(1)} %iota_compare_fusion.1), kind=kOutput, calls=%fused_computation.28 | convolution fusion | flops 77428480 | bytes 3884096 | tf_op jit(solution)/shard_map/nsvgd,ncvd->nsvgc/dot_general | solution.py:56
  272.2 2.3 convert_reduce_fusion.1
  274.5 3.3 fusion.23
  277.9 2.0 copy.70
  283.7 1.9 mul.210
  285.6 1.5 mul.211
  287.1 1.9 mul.207
  289.0 1.5 mul.208
  292.9 10.9 %convolution_convert_fusion = bf16[64,12,5120]{2,0,1:T(8,128)(2,1)} fusion(bf16[384,5120]{1,0:T(8,128)(2,1)} %param.20, f32[64,12,384]{2,0,1:T(8,128)} %div.31, f32[64,12,384]{2,0,1:T(8,128)S(1)} %reshape.278, f32[64,12,384]{2,0,1:T(8,128)} %mul.211, f32[64,12,384]{2,0,1:T(8,128)} %reshape.276, f32[64,12,384]{2,0,1:T(8,128)} %mul.208), kind=kOutput, calls=%fused_computation.10 | convolution fusion | flops 3025305600 | bytes 17694720 | tf_op jit(solution)/shard_map/dot_general | solution.py:173
  303.9 23.7 %copy.95 = bf16[64,12,5120]{0,1,2:T(8,128)(2,1)} copy(bf16[64,12,5120]{2,0,1:T(8,128)(2,1)} %convolution_convert_fusion) | data formatting | bytes 15728640
  327.5 25.8 %reshape.341 = bf16[5120,768]{1,0:T(8,128)(2,1)} reshape(bf16[5120,12,64]{2,1,0:T(8,128)(2,1)} %bitcast.106) | data formatting | bytes 15728640
  353.4 51.9 %reduce-scatter.4.cloned.1.call-done = bf16[640,768]{1,0:T(8,128)(2,1)} async-done(((bf16[5120,768]{1,0:T(8,128)(2,1)}), bf16[640,768]{1,0:T(8,128)(2,1)}) %reduce-scatter.4.cloned.1.call-update) | async-done | bytes 983056
  405.2 4.3 %reshape.342 = bf16[640,12,64]{2,1,0:T(8,128)(2,1)} reshape(bf16[640,768]{1,0:T(8,128)(2,1)} %reduce-scatter.4.cloned.1.call-done) | data formatting | bytes 1966080
  409.5 4.3 %copy.96 = bf16[64,12,640]{2,0,1:T(8,128)(2,1)} copy(bf16[64,12,640]{0,1,2:T(8,128)(2,1)} %bitcast.109) | data formatting | bytes 1966080
  (70 shorter events, 20.1 us)
Async XLA Ops:
  6.5 4.2 copy-start
  24.4 105.2 %all-to-all-start.1 = ((bf16[32,4,128,128]{3,2,1,0:T(8,128)(2,1)}), bf16[32,4,128,128]{3,2,1,0:T(8,128)(2,1)}, u32[]{:S(2)}, u32[]{:S(2)}) async-start(bf16[32,4,128,128]{3,2,1,0:T(8,128)(2,1)} %bitcast.108), calls=%async_computation.1 | async-start | bytes 8388608 | tf_op jit(solution)/shard_map/all_to_all | solution.py:159
  36.6 199.1 %all-gather.2.cloned.1.call-start = ((), (), s32[]{:S(2)}) async-start(), calls=%async_computation.3 | async-start | bytes 8847360 | tf_op jit(solution)/shard_map/all_gather | solution.py:116
  129.7 101.7 %all-to-all-start = ((bf16[32,4,128,128]{3,2,1,0:T(8,128)(2,1)}), bf16[32,4,128,128]{3,2,1,0:T(8,128)(2,1)}, u32[]{:S(2)}, u32[]{:S(2)}) async-start(bf16[32,4,128,128]{3,2,1,0:T(8,128)(2,1)} %bitcast.107), calls=%async_computation | async-start | bytes 8388608 | tf_op jit(solution)/shard_map/all_to_all | solution.py:160
  138.1 267.1 %reduce-scatter.4.cloned.1.call-start = ((), (), s32[]{:S(2)}) async-start(), calls=%async_computation.4 | async-start | bytes 8847360
  138.1 7.0 %copy-start.2 = (s32[2048]{0:T(1024)S(1)}, s32[2048]{0:T(1024)}, u32[]{:S(2)}) copy-start(s32[2048]{0:T(1024)} %param.25) | copy-start | bytes 24580
  235.7 5.0 %copy-start.11 = (f32[5120]{0:T(1024)S(1)}, f32[5120]{0:T(1024)}, u32[]{:S(2)}) copy-start(f32[5120]{0:T(1024)} %param.16) | copy-start | bytes 61444
  235.8 5.5 %copy-start.3 = (bf16[64,12,5120]{2,0,1:T(8,128)(2,1)S(1)}, bf16[64,12,5120]{2,0,1:T(8,128)(2,1)}, u32[]{:S(2)}) copy-start(bf16[64,12,5120]{2,0,1:T(8,128)(2,1)} %all-gather.2.cloned.1.call-done) | copy-start | bytes 23592964
  241.2 5.9 %copy-start.4 = (bf16[5120,384]{0,1:T(8,128)(2,1)S(1)}, bf16[5120,384]{0,1:T(8,128)(2,1)}, u32[]{:S(2)}) copy-start(bf16[5120,384]{0,1:T(8,128)(2,1)} %copy.68) | copy-start | bytes 11796484
  252.3 0.8 copy-start.5
  253.2 2.8 copy-start.10
  266.8 7.7 %copy-start.6 = (bf16[64,128,128]{2,1,0:T(8,128)(2,1)S(1)}, bf16[64,128,128]{2,1,0:T(8,128)(2,1)}, u32[]{:S(2)}) copy-start(bf16[64,128,128]{2,1,0:T(8,128)(2,1)} %gather_fusion.2) | copy-start | bytes 6291460
  279.9 1.5 copy-start.7
  280.0 1.5 copy-start.8
  280.0 1.5 copy-start.9
  405.2 8.6 %copy-start.1 = (bf16[64,128,128]{2,1,0:T(8,128)(2,1)S(1)}, bf16[64,128,128]{2,1,0:T(8,128)(2,1)}, u32[]{:S(2)}) copy-start(bf16[64,128,128]{2,1,0:T(8,128)(2,1)} %param.21) | copy-start | bytes 6291460
Sparse Core Ops, SparseCore 0:
  39.3 51.8 all-gather.1
  353.5 51.6 reduce-scatter.3
where the time goes:
time: 423 us; the launch traced here: 421 us
  waiting for transfers between devices  224 us (53%)
  local copies, waits for them, and re-layouts  104 us (25%)
  matrix products  35.8 us (8%)
  other arithmetic  21.7 us (5%)
  starting transfers between devices  20.7 us (5%)
  between operations  13.7 us (3%)
    all_to_all x1, waiting for transfers between devices, local(): lax.all_to_all(sent_keys, 'group', split_axis=0, concat_axis=0, tiled=True)  92.3 us
    all_to_all x1, waiting for transfers between devices, local(): lax.all_to_all(sent_values, 'group', split_axis=0, concat_axis=0, tiled=T...  79.4 us
    unnamed x30, local copies, waits for them, and re-layouts  66.1 us
    unnamed x3, waiting for transfers between devices  52.6 us
    all_to_all x1, starting transfers between devices, local(): lax.all_to_all(sent_keys, 'group', split_axis=0, concat_axis=0, tiled=True)  12.2 us
    dot_general x1, matrix products, local(): jnp.dot(attended, w_out, preferred_element_type=jnp.float32)  10.9 us
  transfers between devices with their start and end apart: 4, of which 3 were waited for; matrix products, arithmetic and copies ran while one was open for 4% of the time, Pallas kernels for 0%

commit v1 on v0

v1 whole, which is shorter than its diff:
```python
import functools
import math

import jax
import jax.numpy as jnp
import numpy as np
from jax import lax
from jax.experimental import pallas as pl
from jax.experimental.pallas import tpu as pltpu
from jax.sharding import PartitionSpec as P

MESH = pl.DeviceIdType.MESH
HEAD = 128
HEADS = 3
CHUNKS = 3
THETA = 1000000.0
EPS = 1e-06
LOW = -1e30
SCALE = 1.0 / math.sqrt(HEAD)
NT = (((1,), (1,)), ((), ()))
f32 = jnp.float32
bf16 = jnp.bfloat16


def dot(a, b):
    return jnp.dot(a, b, preferred_element_type=f32)


def kernel(
    dims,
    x_hbm, gain_ref, wq_hbm, wk_hbm, wv_hbm, wo_hbm, kc_hbm, vc_hbm,
    cos_hbm, sin_hbm, slot_row, slot_col, kidx, kspan,
    out_hbm,
    xg, w_v, wo_v, k_v, v_v, cos_v, sin_v,
    acc, ssq, qrot, kn, vn, newo, newl,
    sendq, recvq, sendo, recvo, att,
    mine, other, fromp, far, ring_far, side, ring_side, outv,
    local_sem, ag_send, ag_recv, q_send, q_recv, o_send, o_recv,
    p_send, p_recv, far_send, far_recv, side_send, side_recv, out_sem,
):
    ng, nt, steps, part, feat, cap, chunks = dims
    cs = steps // chunks
    rows = cs * part
    half = rows // 2
    hs = cs // 2
    block = cap * cs
    slots = ng * block
    blocks = feat // 128
    nx = nt // 2

    me = lax.axis_index("group")
    t = lax.axis_index("tensor")
    x, core = t // 2, t % 2
    xr, xl, xf = (x + 1) % nx, (x + nx - 1) % nx, (x + 2) % nx
    right, left, partner = xr * 2 + core, xl * 2 + core, x * 2 + 1 - core
    pending = []

    def remote(src, dst, ssem, rsem, dev):
        return pltpu.make_async_remote_copy(
            src_ref=src, dst_ref=dst, send_sem=ssem, recv_sem=rsem,
            device_id=dev, device_id_type=MESH,
        )

    def send(src, dst, ssem, rsem, dev):
        copy = remote(src, dst, ssem, rsem, {"tensor": dev})
        copy.start()
        pending.append(copy)

    def arrived(dst, rsem):
        remote(dst, dst, rsem, rsem, {"tensor": partner}).wait_recv()

    barrier = pltpu.get_barrier_semaphore()
    for dev in (right, left, partner):
        pl.semaphore_signal(barrier, inc=1, device_id={"tensor": dev}, device_id_type=MESH)

    def greet(i, carry):
        pl.semaphore_signal(
            barrier, inc=1, device_id={"group": (me + i) % ng}, device_id_type=MESH
        )
        return carry

    lax.fori_loop(1, ng, greet, 0)

    copies = [
        pltpu.make_async_copy(x_hbm, xg.at[t], local_sem.at[0]),
        pltpu.make_async_copy(cos_hbm, cos_v, local_sem.at[1]),
        pltpu.make_async_copy(sin_hbm, sin_v, local_sem.at[2]),
        pltpu.make_async_copy(kc_hbm, k_v, local_sem.at[3]),
        pltpu.make_async_copy(vc_hbm, v_v, local_sem.at[4]),
    ]
    sem = 5
    w_copies, wo_copies = [], []
    for j in range(nt):
        lo = j * feat
        for ref, at, wide in ((wq_hbm, 0, 384), (wk_hbm, 384, 128), (wv_hbm, 512, 128)):
            w_copies.append(
                pltpu.make_async_copy(
                    ref.at[pl.ds(lo, feat)],
                    w_v.at[j, :, pl.ds(at, wide)],
                    local_sem.at[sem],
                )
            )
            sem += 1
    for j in range(nt):
        wo_copies.append(
            pltpu.make_async_copy(
                wo_hbm.at[:, pl.ds(j * feat, feat)], wo_v.at[j], local_sem.at[sem]
            )
        )
        sem += 1
    for copy in copies[:1] + w_copies + copies[1:] + wo_copies:
        copy.start()
    copies[0].wait()
    pl.semaphore_wait(barrier, 3 + ng - 1)

    def piece(shard, c, lo=0, count=cs):
        return xg.at[shard, pl.ds(c * cs + lo, count)]

    def ag_start(c):
        own = piece(t, c)
        send(own, own, ag_send.at[c, 0], ag_recv.at[c, 0], right)
        send(own, own, ag_send.at[c, 1], ag_recv.at[c, 1], left)
        send(own, own, ag_send.at[c, 2], ag_recv.at[c, 2], partner)

    ag_start(0)
    for copy in w_copies:
        copy.wait()

    def fold(b, carry):
        j, i = b // blocks, b % blocks
        lane = jnp.broadcast_to(gain_ref[pl.ds(b, 1), :], (128, 128))
        tall = jnp.transpose(lane)
        at = pl.ds(pl.multiple_of(i * 128, 128), 128)
        for n in range(5):
            cols = slice(n * 128, (n + 1) * 128)
            w_v[j, at, cols] = (w_v[j, at, cols].astype(f32) * tall).astype(bf16)
        return carry

    lax.fori_loop(0, nt * blocks, fold, 0)

    def shard_dot(shard, c, first=False):
        xs = xg[shard, c * cs:(c + 1) * cs].reshape(rows, feat)
        product = dot(xs, w_v[shard])
        wide = xs.astype(f32)
        squares = wide[:, 0:128] * wide[:, 0:128]
        for i in range(1, blocks):
            part_ = wide[:, i * 128:(i + 1) * 128]
            squares = squares + part_ * part_
        if first:
            acc[...] = product
            ssq[...] = squares
        else:
            acc[...] += product
            ssq[...] += squares

    def shard_of(xi, co):
        return xi * 2 + co

    def project(c):
        shard_dot(t, c, True)
        arrived(piece(partner, c), ag_recv.at[c, 2])
        shard_dot(partner, c)
        sl, sr, sf = shard_of(xl, core), shard_of(xr, core), shard_of(xf, core)
        arrived(piece(sl, c), ag_recv.at[c, 0])
        send(piece(sl, c, 0, hs), piece(sl, c, 0, hs), ag_send.at[c, 3], ag_recv.at[c, 3], right)
        send(piece(sl, c), piece(sl, c), ag_send.at[c, 4], ag_recv.at[c, 4], partner)
        arrived(piece(sr, c), ag_recv.at[c, 1])
        send(piece(sr, c, hs, hs), piece(sr, c, hs, hs), ag_send.at[c, 5], ag_recv.at[c, 5], left)
        send(piece(sr, c), piece(sr, c), ag_send.at[c, 6], ag_recv.at[c, 6], partner)
        if c + 1 < chunks:
            ag_start(c + 1)
        shard_dot(sl, c)
        shard_dot(sr, c)
        arrived(piece(sf, c, 0, hs), ag_recv.at[c, 3])
        send(piece(sf, c, 0, hs), piece(sf, c, 0, hs), ag_send.at[c, 7], ag_recv.at[c, 7], partner)
        arrived(piece(sf, c, hs, hs), ag_recv.at[c, 5])
        send(piece(sf, c, hs, hs), piece(sf, c, hs, hs), ag_send.at[c, 8], ag_recv.at[c, 8], partner)
        shard_dot(sf, c)
        pl_, pr, pf = shard_of(xl, 1 - core), shard_of(xr, 1 - core), shard_of(xf, 1 - core)
        arrived(piece(pl_, c), ag_recv.at[c, 4])
        shard_dot(pl_, c)
        arrived(piece(pr, c), ag_recv.at[c, 6])
        shard_dot(pr, c)
        arrived(piece(pf, c, 0, hs), ag_recv.at[c, 7])
        arrived(piece(pf, c, hs, hs), ag_recv.at[c, 8])
        shard_dot(pf, c)
        if c == 0:
            copies[1].wait()
            copies[2].wait()
        mean = jnp.sum(ssq[...], axis=1, keepdims=True) * (1.0 / (nt * feat))
        inv = lax.rsqrt(mean + EPS)
        here = slice(c * rows, (c + 1) * rows)
        cos, sin = cos_v[here], sin_v[here]

        def turn(v):
            v = v * inv
            return (v * cos + pltpu.roll(v, 64, 1) * sin).astype(bf16)

        for h in range(HEADS):
            qrot[c, :, h * 128:(h + 1) * 128] = turn(acc[:, h * 128:(h + 1) * 128])
        kn[here] = turn(acc[:, 384:512])
        vn[here] = (acc[:, 512:640] * inv).astype(bf16)

    def route(c):
        pick = lax.broadcasted_iota(jnp.int32, (slots, rows), 0) == slot_row[...]
        pick = pick.astype(f32).astype(bf16)
        moved = dot(pick, qrot[c]).astype(bf16)
        sendq[c] = moved.reshape(ng, block, 384)

        def go(i, carry):
            g = (me + i) % ng
            remote(
                sendq.at[c, g], recvq.at[c, me], q_send.at[c], q_recv.at[c, me], {"group": g}
            ).start()
            return carry

        lax.fori_loop(1, ng, go, 0)
        recvq[c, me] = sendq[c, me]

    def fresh(c):
        keys = (c + 1) * rows
        row = lax.broadcasted_iota(jnp.int32, (rows, keys), 0)
        col = lax.broadcasted_iota(jnp.int32, (rows, keys), 1)
        same = (row % part) == (col % part)
        causal = (col // part) <= (row // part + c * cs)
        ok = same & causal
        for h in range(HEADS):
            lanes = slice(h * 128, (h + 1) * 128)
            s = lax.dot_general(qrot[c, :, lanes], kn[0:keys], NT, preferred_element_type=f32)
            s = jnp.where(ok, s * SCALE, LOW)
            m = jnp.max(s, axis=1, keepdims=True)
            w = jnp.exp(s - m).astype(bf16)
            total = jnp.sum(w.astype(f32), axis=1, keepdims=True)
            o = dot(w, vn[0:keys])
            newo[c, :, lanes] = o / total
            newl[c, h] = jnp.broadcast_to(m + jnp.log(total), (rows, 128))

    lane3 = lax.broadcasted_iota(jnp.int32, (HEADS * block, 128), 1)
    rank3 = (lax.broadcasted_iota(jnp.int32, (HEADS * block, 128), 0) % block) // cs

    def cached(c, src):
        got = recvq[c, src]
        q = jnp.concatenate([got[:, h * 128:(h + 1) * 128] for h in range(HEADS)], axis=0)
        s = None
        slot = [kidx[src * cap + r] for r in range(cap)]
        for r in range(cap):
            one = lax.dot_general(q, k_v[slot[r]], NT, preferred_element_type=f32)
            one = jnp.where(lane3 < kspan[src * cap + r], one * SCALE, LOW)
            s = one if s is None else jnp.where(rank3 == r, one, s)
        m = jnp.max(s, axis=1, keepdims=True)
        w = jnp.exp(s - m).astype(bf16).astype(f32)
        total = jnp.sum(w, axis=1, keepdims=True)
        o = None
        for r in range(cap):
            one = dot(jnp.where(rank3 == r, w, 0.0).astype(bf16), v_v[slot[r]])
            o = one if o is None else o + one
        o = (o / total).astype(bf16)
        lse = jnp.broadcast_to(m + jnp.log(total), (HEADS * block, 128))
        hi = lse.astype(bf16).astype(f32)
        mid = (lse - hi).astype(bf16).astype(f32)
        lo = (lse - hi - mid).astype(bf16).astype(f32)
        kind = lane3 % 4
        terms = jnp.where(kind == 0, hi, jnp.where(kind == 1, mid, jnp.where(kind == 2, lo, 0.0)))
        head_lane = lane3[0:block] // 4
        stat = jnp.zeros((block, 128), f32)
        for h in range(HEADS):
            stat = jnp.where(head_lane == h, terms[h * block:(h + 1) * block], stat)
        both = [o[h * block:(h + 1) * block] for h in range(HEADS)] + [stat.astype(bf16)]
        return jnp.concatenate(both, axis=1)

    def serve(c):
        recvo[c, me] = cached(c, me)

        def go(i, carry):
            src = (me + ng - i) % ng
            remote(
                recvq.at[c, src], recvq.at[c, src], q_send.at[c], q_recv.at[c, src],
                {"group": src},
            ).wait_recv()
            sendo[c, src] = cached(c, src)
            remote(
                sendo.at[c, src], recvo.at[c, me], o_send.at[c], o_recv.at[c], {"group": src}
            ).start()
            return carry

        lax.fori_loop(1, ng, go, 0)

    def combine(c):
        span = pl.ds(0, ng - 1)
        remote(
            sendo.at[c, span], recvo.at[c, span], o_send.at[c], o_recv.at[c],
            {"group": (me + 1) % ng},
        ).wait_recv()
        pick = lax.broadcasted_iota(jnp.int32, (rows, slots), 1) == slot_col[...]
        pick = pick.astype(f32).astype(bf16)
        back = dot(pick, recvo[c].reshape(slots, 512))
        lane = lax.broadcasted_iota(jnp.int32, (rows, 128), 1) // 4
        stat = back[:, 384:512]
        for h in range(HEADS):
            lanes = slice(h * 128, (h + 1) * 128)
            cache_l = jnp.sum(jnp.where(lane == h, stat, 0.0), axis=1, keepdims=True)
            gap = newl[c, h] - cache_l
            a = 1.0 / (1.0 + jnp.exp(gap))
            b = 1.0 / (1.0 + jnp.exp(-gap))
            att[:, lanes] = (back[:, lanes] * a + newo[c, :, lanes] * b).astype(bf16)

    order = (xf, xr, xl, x)

    def give(c):
        for n, xi in enumerate(order):
            other[c, n] = dot(att[...], wo_v[shard_of(xi, 1 - core)]).astype(bf16)
            send(other.at[c, n], fromp.at[c, n], p_send.at[c, n], p_recv.at[c, n], partner)
        for n, xi in enumerate(order):
            mine[c, n] = dot(att[...], wo_v[shard_of(xi, core)]).astype(bf16)

    top, low = slice(0, half), slice(half, rows)

    def chip_sum(c, n, at):
        return mine[c, n, at].astype(f32) + fromp[c, n, at].astype(f32)

    def spread(c):
        arrived(fromp.at[c, 0], p_recv.at[c, 0])
        far[c] = chip_sum(c, 0, slice(0, rows)).astype(bf16)
        send(far.at[c, pl.ds(0, half)], ring_far.at[c, 0], far_send.at[c, 0], far_recv.at[c, 0], right)
        send(far.at[c, pl.ds(half, half)], ring_far.at[c, 1], far_send.at[c, 1], far_recv.at[c, 1], left)
        arrived(fromp.at[c, 1], p_recv.at[c, 1])
        side[c, 0, 1] = chip_sum(c, 1, low).astype(bf16)
        send(side.at[c, 0, 1], ring_side.at[c, 0, 1], side_send.at[c, 0, 1], side_recv.at[c, 0, 1], right)
        arrived(fromp.at[c, 2], p_recv.at[c, 2])
        side[c, 1, 0] = chip_sum(c, 2, top).astype(bf16)
        send(side.at[c, 1, 0], ring_side.at[c, 1, 0], side_send.at[c, 1, 0], side_recv.at[c, 1, 0], left)

    def relay(c):
        arrived(ring_far.at[c, 0], far_recv.at[c, 0])
        side[c, 0, 0] = (chip_sum(c, 1, top) + ring_far[c, 0].astype(f32)).astype(bf16)
        send(side.at[c, 0, 0], ring_side.at[c, 0, 0], side_send.at[c, 0, 0], side_recv.at[c, 0, 0], right)
        arrived(ring_far.at[c, 1], far_recv.at[c, 1])
        side[c, 1, 1] = (chip_sum(c, 2, low) + ring_far[c, 1].astype(f32)).astype(bf16)
        send(side.at[c, 1, 1], ring_side.at[c, 1, 1], side_send.at[c, 1, 1], side_recv.at[c, 1, 1], left)

    outs = []

    def finish(c):
        arrived(fromp.at[c, 3], p_recv.at[c, 3])
        for n in (1, 0):
            for s in (1, 0) if n == 0 else (0, 1):
                arrived(ring_side.at[c, s, n], side_recv.at[c, s, n])
            at = slice(n * half, (n + 1) * half)
            total = chip_sum(c, 3, at)
            total = total + ring_side[c, 0, n].astype(f32) + ring_side[c, 1, n].astype(f32)
            outv[c * cs + n * hs:c * cs + (n + 1) * hs] = total.astype(bf16).reshape(hs, part, feat)
        copy = pltpu.make_async_copy(
            outv.at[pl.ds(c * cs, cs)], out_hbm.at[pl.ds(c * cs, cs)], out_sem.at[c]
        )
        copy.start()
        outs.append(copy)

    for c in range(chunks):
        project(c)
        route(c)
        fresh(c)
        if c == 0:
            copies[3].wait()
            copies[4].wait()
        if c >= 1:
            serve(c - 1)
        if c >= 2:
            combine(c - 2)
            if c == 2:
                for copy in wo_copies:
                    copy.wait()
            give(c - 2)
            spread(c - 2)
    last = chunks - 1
    if chunks < 3:
        for copy in wo_copies:
            copy.wait()
    serve(last)
    if chunks >= 3:
        relay(last - 2)
    if chunks >= 2:
        combine(last - 1)
        give(last - 1)
        spread(last - 1)
    if chunks >= 3:
        finish(last - 2)
    if chunks >= 2:
        relay(last - 1)
    combine(last)
    give(last)
    spread(last)
    if chunks >= 2:
        finish(last - 1)
    relay(last)
    finish(last)

    for copy in pending:
        copy.wait_send()
    span = pl.ds(0, ng - 1)
    for c in range(chunks):
        remote(
            sendq.at[c, span], recvq.at[c, span], q_send.at[c], q_recv.at[c, 0],
            {"group": (me + 1) % ng},
        ).wait_send()
        remote(
            sendo.at[c, span], recvo.at[c, span], o_send.at[c], o_recv.at[c],
            {"group": (me + 1) % ng},
        ).wait_send()
    for copy in outs:
        copy.wait()


def call(dims, *args):
    ng, nt, steps, part, feat, cap, chunks = dims
    cs = steps // chunks
    rows = cs * part
    block = cap * cs
    any_ = pl.BlockSpec(memory_space=pl.ANY)
    vmem = pl.BlockSpec(memory_space=pltpu.VMEM)
    smem = pl.BlockSpec(memory_space=pltpu.SMEM)
    dma = pltpu.SemaphoreType.DMA
    V = pltpu.VMEM
    scratch = [
        V((nt, steps, part, feat), bf16), V((nt, feat, 640), bf16), V((nt, 384, feat), bf16),
        V((part, 128, 128), bf16), V((part, 128, 128), bf16),
        V((steps * part, 128), f32), V((steps * part, 128), f32),
        V((rows, 640), f32), V((rows, 128), f32), V((chunks, rows, 384), bf16),
        V((steps * part, 128), bf16), V((steps * part, 128), bf16),
        V((chunks, rows, 384), f32), V((chunks, HEADS, rows, 128), f32),
        V((chunks, ng, block, 384), bf16), V((chunks, ng, block, 384), bf16),
        V((chunks, ng, block, 512), bf16), V((chunks, ng, block, 512), bf16),
        V((rows, 384), bf16),
        V((chunks, 4, rows, feat), bf16), V((chunks, 4, rows, feat), bf16),
        V((chunks, 4, rows, feat), bf16),
        V((chunks, rows, feat), bf16), V((chunks, 2, rows // 2, feat), bf16),
        V((chunks, 2, 2, rows // 2, feat), bf16), V((chunks, 2, 2, rows // 2, feat), bf16),
        V((steps, part, feat), bf16),
        dma((5 + 4 * nt,)), dma((chunks, 9)), dma((chunks, 9)),
        dma((chunks,)), dma((chunks, ng)), dma((chunks,)), dma((chunks,)),
        dma((chunks, 4)), dma((chunks, 4)), dma((chunks, 2)), dma((chunks, 2)),
        dma((chunks, 2, 2)), dma((chunks, 2, 2)), dma((chunks,)),
    ]
    return pl.pallas_call(
        functools.partial(kernel, dims),
        out_shape=jax.ShapeDtypeStruct((steps, part, feat), bf16),
        in_specs=[any_, vmem] + [any_] * 8 + [vmem, vmem, smem, smem],
        out_specs=any_,
        scratch_shapes=scratch,
        compiler_params=pltpu.CompilerParams(
            collective_id=0, has_side_effects=True, vmem_limit_bytes=62 * 1024 * 1024
        ),
    )(*args)


def local(
    states, norm_gain, w_query, w_key, w_value, w_out, key_cache, value_cache,
    ancestor_group, ancestor_slot, lengths,
):
    part, steps, feat = states.shape
    ng, nt = lax.axis_size("group"), lax.axis_size("tensor")
    cap = max(2, (2 * part + ng - 1) // ng)
    dims = (ng, nt, steps, part, feat, cap, CHUNKS)
    cs = steps // CHUNKS
    me = lax.axis_index("group")

    sources = ancestor_group[:, 0].reshape(ng, part)
    places = ancestor_slot.reshape(ng, part)
    spans = lengths.reshape(ng, part)
    asked = sources == me
    rank = jnp.cumsum(asked.astype(jnp.int32), axis=1) - 1
    chosen = asked[:, None, :] & (rank[:, None, :] == jnp.arange(cap)[None, :, None])
    kidx = jnp.sum(jnp.where(chosen, places[:, None, :], 0), axis=2).reshape(-1)
    my_lengths = lax.dynamic_index_in_dim(spans, me, 0, keepdims=False)
    own_place = (kidx[:, None] == jnp.arange(part)[None, :])
    kspan = jnp.sum(jnp.where(own_place, my_lengths[None, :], 0), axis=1)
    mine = lax.dynamic_index_in_dim(sources, me, 0, keepdims=False)
    my_place = lax.dynamic_index_in_dim(places, me, 0, keepdims=False)
    earlier = jnp.arange(part)[None, :] < jnp.arange(part)[:, None]
    my_rank = jnp.sum((mine[:, None] == mine[None, :]) & earlier, axis=1)
    slot = mine * cap + my_rank
    target = (slot[None, :] * cs + jnp.arange(cs, dtype=jnp.int32)[:, None]).reshape(-1)
    my_span = jnp.take(lengths, mine * part + my_place)
    position = (my_span[None, :] + jnp.arange(steps, dtype=jnp.int32)[:, None]).reshape(-1)
    index = jnp.arange(64, dtype=f32)
    inverse = THETA ** (-2.0 * index / 128)
    angles = position.astype(f32)[:, None] * inverse
    cos, sin = jnp.cos(angles), jnp.sin(angles)
    cos = jnp.concatenate([cos, cos], axis=1)
    sin = jnp.concatenate([-sin, sin], axis=1)

    out = call(
        dims,
        jnp.transpose(states, (1, 0, 2)),
        norm_gain.reshape(-1, 128),
        w_query, w_key, w_value, w_out, key_cache, value_cache,
        cos, sin,
        target[None, :], target[:, None],
        kidx.astype(jnp.int32), kspan.astype(jnp.int32),
    )
    return jnp.transpose(out, (1, 0, 2))


def solution(mesh):
    in_specs = (
        P("group", None, "tensor"),
        P(),
        P(None, "tensor"),
        P(None, "tensor"),
        P(None, "tensor"),
        P("tensor", None),
        P("group", None, "tensor"),
        P("group", None, "tensor"),
        P(),
        P(),
        P(),
    )
    out_specs = P("group", None, "tensor")
    return jax.shard_map(local, mesh=mesh, in_specs=in_specs, out_specs=out_specs, check_vma=False)
```

time: 423 us -> 148 us (0.35)
  waiting for transfers between devices: 224 us -> 0 us
  Pallas kernels: 0 us -> 136 us
  local copies, waits for them, and re-layouts: 104 us -> 6.86 us
  matrix products: 35.8 us -> 0 us
  starting transfers between devices: 20.7 us -> 0 us
  other arithmetic: 21.7 us -> 5.2 us
  between operations: 13.7 us -> 0.07 us
    all_to_all x2 -> x0, waiting for transfers between devices: 172 us -> none  [the longest x1 92.3 us: local(): lax.all_to_all(sent_keys, 'group', split_axis=0, concat_axis=0, tiled=True)]
    pallas_call x0 -> x1, Pallas kernels: none -> 136 us  [call(): pl.pallas_call(functools.partial(kernel, dims), out_shape=jax.ShapeDtypeS...]
    unnamed x30 -> x6, local copies, waits for them, and re-layouts: 66.1 us -> 2.75 us
    unnamed x3 -> x0, waiting for transfers between devices: 52.6 us -> none
    dot_general x8 -> x0, matrix products: 35.8 us -> none  [the longest x1 10.9 us: local(): jnp.dot(attended, w_out, preferred_element_type=jnp.float32)]
    all_to_all x2 -> x0, starting transfers between devices: 20.6 us -> none  [the longest x1 12.2 us: local(): lax.all_to_all(sent_keys, 'group', split_axis=0, concat_axis=0, tiled=True)]
    gather x5 -> x1, local copies, waits for them, and re-layouts: 17.3 us -> 1.47 us  [local(): my_span = jnp.take(lengths, mine * part + my_place)]
    reduce_sum x5 -> x3, other arithmetic: 8.95 us -> 0.93 us  [the longest x1 0.6 us: local(): kspan = jnp.sum(jnp.where(own_place, my_lengths[None, :], 0), axis=1)]
  transfers between devices with their start and end apart: 4 -> 0, of which waited for: 3 -> 0; matrix products, arithmetic and copies ran while one was open for 4% -> 0% of each run, Pallas kernels for 0% -> 0%
where the time goes in v1:
time: 148 us
  Pallas kernels  136 us (92%)
  local copies, waits for them, and re-layouts  6.86 us (5%)
  other arithmetic  5.2 us (4%)
    pallas_call x1, Pallas kernels, call(): pl.pallas_call(functools.partial(kernel, dims), out_shape=jax.ShapeDtypeS...  136 us

profile of v1, /device:TPU:1, one launch (start us, length us, event | category | flops | bytes accessed | tf_op | source)
XLA Modules:
  0.0 147.9 jit_solution(2754669649980204475)
XLA Ops:
  0.0 0.0 copy-start
  0.0 0.5 broadcast.89
  0.5 1.4 reduce.3
  1.9 0.1 reshape_squeeze.3
  2.0 0.8 reshape.141
  2.7 1.5 gather_fusion
  4.2 0.1 convert_element_type.21
  4.3 1.5 fusion
  5.8 1.2 pad_maximum_fusion
  6.9 0.2 convert_reduce_fusion
  7.1 0.0 copy-done
  7.1 0.1 reshape.143
  7.2 0.2 reduce_window_sum.11
  7.5 0.2 select_reduce_fusion
  7.6 0.1 copy.13
  7.7 0.1 reshape.142.kidx
  7.8 0.0 copy-start.1
  7.8 0.6 select_reduce_fusion.1.kspan
  8.4 0.8 add.127.slot_col
  9.2 0.7 add.125.slot_row
  9.9 0.0 copy-done.1
  9.9 135.7 %shard_map.109 = bf16[12,64,640]{2,1,0:T(8,128)(2,1)} custom-call(bf16[12,64,640]{2,1,0:T(8,128)(2,1)} %bitcast.27, f32[40,128]{1,0:T(8,128)} %bitcast.28, bf16[5120,384]{1,0:T(8,128)(2,1)} %wq_hbm.1, bf16[5120,128]{1,0:T(8,128)(2,1)} %wk_hbm.1, bf16[5120,128]{1,0:T(8,128)(2,1)} %wv_hbm.1, bf16[384,5120]{1,0:T(8,128)(2,1)} %wo_hbm.1, ...), custom_call_target="tpu_custom_call" | custom-call | tf_op jit(solution)/shard_map/pallas_call | solution.py:443
  145.6 2.2 %copy.16 = bf16[64,12,640]{2,0,1:T(8,128)(2,1)} copy(bf16[64,12,640]{2,0,1:T(8,128)(2,1)} %bitcast.26) | data formatting | bytes 1966080
  (10 shorter events, 0.1 us)
Async XLA Ops:
  0.0 7.1 %copy-start = (s32[2048]{0:T(1024)S(1)}, s32[2048]{0:T(1024)}, u32[]{:S(2)}) copy-start(s32[2048]{0:T(1024)} %param.21) | copy-start | bytes 24580
  7.8 2.1 %copy-start.1 = (s32[128]{0:T(128)}, s32[128]{0:T(128)S(1)}, u32[]{:S(2)}) copy-start(s32[128]{0:T(128)S(1)} %reshape.142.kidx) | copy-start | bytes 1540

commit v2 on v1

--- a/solution.py
+++ b/solution.py
@@ -13,6 +13,12 @@
 HEAD = 128
 HEADS = 3
 CHUNKS = 3
+ORDER = (
+    "A0", "B0", "R0", "A1", "s0", "B1", "R1", "t0", "F0", "A2",
+    "s1", "B2", "R2", "t1", "F1", "C0", "V0", "P0", "s2", "L0",
+    "t2", "F2", "C1", "V1", "P1", "N0", "L1", "C2", "V2", "P2",
+    "N1", "L2", "N2",
+)
 THETA = 1000000.0
 EPS = 1e-06
 LOW = -1e30
@@ -29,13 +35,13 @@
 def kernel(
     dims,
     x_hbm, gain_ref, wq_hbm, wk_hbm, wv_hbm, wo_hbm, kc_hbm, vc_hbm,
-    cos_hbm, sin_hbm, slot_row, slot_col, kidx, kspan,
+    group_ref, place_ref, length_ref, lengths_s, turns_ref,
     out_hbm,
-    xg, w_v, wo_v, k_v, v_v, cos_v, sin_v,
+    xg, w_v, wo_v, k_v, v_v, cos_v, sin_v, slot_row, slot_col, table_v, table_s,
     acc, ssq, qrot, kn, vn, newo, newl,
-    sendq, recvq, sendo, recvo, att,
+    sendq, recvq, sendo, recvo, sendl, recvl, att,
     mine, other, fromp, far, ring_far, side, ring_side, outv,
-    local_sem, ag_send, ag_recv, q_send, q_recv, o_send, o_recv,
+    local_sem, ag_send, ag_recv, q_send, q_recv, o_send, o_recv, l_send, l_recv,
     p_send, p_recv, far_send, far_recv, side_send, side_recv, out_sem,
 ):
     ng, nt, steps, part, feat, cap, chunks = dims
@@ -69,6 +75,9 @@
     def arrived(dst, rsem):
         remote(dst, dst, rsem, rsem, {"tensor": partner}).wait_recv()
 
+    first = pltpu.make_async_copy(x_hbm, xg.at[t], local_sem.at[0])
+    first.start()
+
     barrier = pltpu.get_barrier_semaphore()
     for dev in (right, left, partner):
         pl.semaphore_signal(barrier, inc=1, device_id={"tensor": dev}, device_id_type=MESH)
@@ -82,13 +91,10 @@
     lax.fori_loop(1, ng, greet, 0)
 
     copies = [
-        pltpu.make_async_copy(x_hbm, xg.at[t], local_sem.at[0]),
-        pltpu.make_async_copy(cos_hbm, cos_v, local_sem.at[1]),
-        pltpu.make_async_copy(sin_hbm, sin_v, local_sem.at[2]),
-        pltpu.make_async_copy(kc_hbm, k_v, local_sem.at[3]),
-        pltpu.make_async_copy(vc_hbm, v_v, local_sem.at[4]),
+        pltpu.make_async_copy(kc_hbm, k_v, local_sem.at[1]),
+        pltpu.make_async_copy(vc_hbm, v_v, local_sem.at[2]),
     ]
-    sem = 5
+    sem = 3
     w_copies, wo_copies = [], []
     for j in range(nt):
         lo = j * feat
@@ -108,9 +114,7 @@
             )
         )
         sem += 1
-    for copy in copies[:1] + w_copies + copies[1:] + wo_copies:
-        copy.start()
-    copies[0].wait()
+    first.wait()
     pl.semaphore_wait(barrier, 3 + ng - 1)
 
     def piece(shard, c, lo=0, count=cs):
@@ -123,6 +127,8 @@
         send(own, own, ag_send.at[c, 2], ag_recv.at[c, 2], partner)
 
     ag_start(0)
+    for copy in w_copies:
+        copy.start()
     for copy in w_copies:
         copy.wait()
 
@@ -137,6 +143,74 @@
         return carry
 
     lax.fori_loop(0, nt * blocks, fold, 0)
+
+    def count(shape, axis):
+        return lax.broadcasted_iota(jnp.int32, shape, axis)
+
+    two = 128 // part
+    lines = ng // two
+    row_i, col_i = count((128, 128), 0), count((128, 128), 1)
+    lane_l = count((lines, 128), 1)
+    asked = jnp.where(group_ref[...] == me, 1, 0)
+    within = lane_l % part
+    rank = asked
+    hop = 1
+    while hop < part:
+        rank = rank + jnp.where(within >= hop, pltpu.roll(rank, hop, 1), 0)
+        hop *= 2
+    table = jnp.zeros((lines, 128), jnp.int32)
+    for r in range(cap):
+        found = jnp.where((asked == 1) & (rank == r + 1), place_ref[...], 0)
+        hop = 1
+        while hop < part:
+            found = found + jnp.where(within >= hop, pltpu.roll(found, hop, 1), 0)
+            hop *= 2
+        for n in range(two):
+            to = n * cap + r
+            moved = pltpu.roll(found, (to - (n + 1) * part + 1) % 128, 1)
+            table = jnp.where(lane_l == to, moved, table)
+    table_v[...] = table
+    table_copy = pltpu.make_async_copy(table_v, table_s, local_sem.at[3 + 4 * nt])
+    table_copy.start()
+
+    def own_line(ref):
+        line = ref[pl.ds(me // two, 1), :].astype(f32)
+        best = line
+        for n in range(1, two):
+            best = jnp.where(me % two == n, pltpu.roll(line, 128 - n * part, 1), best)
+        return best
+
+    wide_group = jnp.broadcast_to(own_line(group_ref), (128, 128))
+    wide_place = jnp.broadcast_to(own_line(place_ref), (128, 128))
+    tall_group, tall_place = jnp.transpose(wide_group), jnp.transpose(wide_place)
+    match = (wide_group == tall_group).astype(f32)
+    row_rank = jnp.sum(jnp.where(row_i < col_i, match, 0.0), axis=0, keepdims=True)
+    col_rank = jnp.sum(jnp.where(col_i < row_i, match, 0.0), axis=1, keepdims=True)
+    row_slot = (wide_group[0:1] * cap + row_rank) * cs
+    col_slot = (tall_group * cap + col_rank) * cs
+    row_slot = jnp.where(count((1, 128), 1) < part, row_slot, 0.0)
+    for n in range(1, two):
+        row_slot = row_slot + jnp.where(
+            count((1, 128), 1) // part == n, pltpu.roll(row_slot, n * part, 1), 0.0
+        )
+    for n in range(cs // two):
+        ahead = row_slot + (count((1, 128), 1) // part + n * two).astype(f32)
+        slot_row[:, n * 128:(n + 1) * 128] = ahead.astype(jnp.int32)
+    for n in range(cs):
+        slot_col[n * part:(n + 1) * part] = (col_slot[0:part] + n).astype(jnp.int32)
+    which = (tall_group * (1.0 / two)).astype(jnp.int32)
+    rest = tall_group.astype(jnp.int32) - which * two
+    line_of = (which[0:part, 0:lines] == count((part, lines), 1)).astype(f32).astype(bf16)
+    near = dot(line_of, length_ref[...].astype(f32).astype(bf16))
+    at_lane = rest * part + tall_place.astype(jnp.int32)
+    near = jnp.where(count((part, 128), 1) == at_lane[0:part], near, 0.0)
+    span_col = jnp.sum(near, axis=1, keepdims=True)
+    angle = span_col * turns_ref[0:1]
+    cos_a, sin_a = jnp.cos(angle), jnp.sin(angle)
+    for n in range(steps):
+        cos_b, sin_b = turns_ref[8 + n:9 + n], turns_ref[8 + steps + n:9 + steps + n]
+        cos_v[n * part:(n + 1) * part] = cos_a * cos_b - sin_a * sin_b
+        sin_v[n * part:(n + 1) * part] = (sin_a * cos_b + cos_a * sin_b) * turns_ref[1:2]
 
     def shard_dot(shard, c, first=False):
         xs = xg[shard, c * cs:(c + 1) * cs].reshape(rows, feat)
@@ -156,11 +230,12 @@
     def shard_of(xi, co):
         return xi * 2 + co
 
+    sl, sr, sf = shard_of(xl, core), shard_of(xr, core), shard_of(xf, core)
+
     def project(c):
         shard_dot(t, c, True)
         arrived(piece(partner, c), ag_recv.at[c, 2])
         shard_dot(partner, c)
-        sl, sr, sf = shard_of(xl, core), shard_of(xr, core), shard_of(xf, core)
         arrived(piece(sl, c), ag_recv.at[c, 0])
         send(piece(sl, c, 0, hs), piece(sl, c, 0, hs), ag_send.at[c, 3], ag_recv.at[c, 3], right)
         send(piece(sl, c), piece(sl, c), ag_send.at[c, 4], ag_recv.at[c, 4], partner)
@@ -171,6 +246,11 @@
             ag_start(c + 1)
         shard_dot(sl, c)
         shard_dot(sr, c)
+
+    def project_rest(c):
+        if c == 0:
+            for copy in copies + wo_copies:
+                copy.start()
         arrived(piece(sf, c, 0, hs), ag_recv.at[c, 3])
         send(piece(sf, c, 0, hs), piece(sf, c, 0, hs), ag_send.at[c, 7], ag_recv.at[c, 7], partner)
         arrived(piece(sf, c, hs, hs), ag_recv.at[c, 5])
@@ -184,9 +264,6 @@
         arrived(piece(pf, c, 0, hs), ag_recv.at[c, 7])
         arrived(piece(pf, c, hs, hs), ag_recv.at[c, 8])
         shard_dot(pf, c)
-        if c == 0:
-            copies[1].wait()
-            copies[2].wait()
         mean = jnp.sum(ssq[...], axis=1, keepdims=True) * (1.0 / (nt * feat))
         inv = lax.rsqrt(mean + EPS)
         here = slice(c * rows, (c + 1) * rows)
@@ -201,14 +278,18 @@
         kn[here] = turn(acc[:, 384:512])
         vn[here] = (acc[:, 512:640] * inv).astype(bf16)
 
+    def offset(i):
+        away, odd = (i + 1) // 2, i % 2
+        return odd * away + (1 - odd) * (ng - away)
+
     def route(c):
-        pick = lax.broadcasted_iota(jnp.int32, (slots, rows), 0) == slot_row[...]
+        pick = count((slots, rows), 0) == slot_row[...]
         pick = pick.astype(f32).astype(bf16)
         moved = dot(pick, qrot[c]).astype(bf16)
         sendq[c] = moved.reshape(ng, block, 384)
 
         def go(i, carry):
-            g = (me + i) % ng
+            g = (me + offset(i)) % ng
             remote(
                 sendq.at[c, g], recvq.at[c, me], q_send.at[c], q_recv.at[c, me], {"group": g}
             ).start()
@@ -235,55 +316,96 @@
             newo[c, :, lanes] = o / total
             newl[c, h] = jnp.broadcast_to(m + jnp.log(total), (rows, 128))
 
-    lane3 = lax.broadcasted_iota(jnp.int32, (HEADS * block, 128), 1)
-    rank3 = (lax.broadcasted_iota(jnp.int32, (HEADS * block, 128), 0) % block) // cs
-
-    def cached(c, src):
-        got = recvq[c, src]
-        q = jnp.concatenate([got[:, h * 128:(h + 1) * 128] for h in range(HEADS)], axis=0)
-        s = None
-        slot = [kidx[src * cap + r] for r in range(cap)]
-        for r in range(cap):
-            one = lax.dot_general(q, k_v[slot[r]], NT, preferred_element_type=f32)
-            one = jnp.where(lane3 < kspan[src * cap + r], one * SCALE, LOW)
-            s = one if s is None else jnp.where(rank3 == r, one, s)
+    many = min(4, ng)
+    block3 = HEADS * block
+    tall3 = many * block3
+    lane3 = count((tall3, 128), 1)
+    rank3 = (count((tall3, 128), 0) % block) // cs
+    wide_l = recvl.shape[3]
+    lane_s = count((tall3, wide_l), 1)
+    row3 = count((tall3, wide_l), 0) % block3
+
+    def cached(c, sources):
+        slot = [
+            [
+                jnp.clip(table_s[src // two, (src % two) * cap + r], 0, part - 1)
+                for r in range(cap)
+            ]
+            for src in sources
+        ]
+        scores = []
+        for src, own in zip(sources, slot):
+            got = recvq[c, src]
+            q = jnp.concatenate([got[:, h * 128:(h + 1) * 128] for h in range(HEADS)], axis=0)
+            keys = jnp.concatenate([k_v[a] for a in own], axis=0)
+            s = lax.dot_general(q, keys, NT, preferred_element_type=f32) * SCALE
+            best = None
+            for r, a in enumerate(own):
+                length = lengths_s[me * part + a]
+                one = jnp.where(lane3[0:block3] < length, s[:, r * 128:(r + 1) * 128], LOW)
+                best = one if best is None else jnp.where(rank3[0:block3] == r, one, best)
+            scores.append(best)
+        s = jnp.concatenate(scores, axis=0)
         m = jnp.max(s, axis=1, keepdims=True)
         w = jnp.exp(s - m).astype(bf16).astype(f32)
         total = jnp.sum(w, axis=1, keepdims=True)
-        o = None
-        for r in range(cap):
-            one = dot(jnp.where(rank3 == r, w, 0.0).astype(bf16), v_v[slot[r]])
-            o = one if o is None else o + one
-        o = (o / total).astype(bf16)
-        lse = jnp.broadcast_to(m + jnp.log(total), (HEADS * block, 128))
-        hi = lse.astype(bf16).astype(f32)
-        mid = (lse - hi).astype(bf16).astype(f32)
-        lo = (lse - hi - mid).astype(bf16).astype(f32)
-        kind = lane3 % 4
-        terms = jnp.where(kind == 0, hi, jnp.where(kind == 1, mid, jnp.where(kind == 2, lo, 0.0)))
-        head_lane = lane3[0:block] // 4
-        stat = jnp.zeros((block, 128), f32)
-        for h in range(HEADS):
-            stat = jnp.where(head_lane == h, terms[h * block:(h + 1) * block], stat)
-        both = [o[h * block:(h + 1) * block] for h in range(HEADS)] + [stat.astype(bf16)]
-        return jnp.concatenate(both, axis=1)
-
-    def serve(c):
-        recvo[c, me] = cached(c, me)
-
-        def go(i, carry):
-            src = (me + ng - i) % ng
+        w = jnp.concatenate([jnp.where(rank3 == r, w, 0.0).astype(bf16) for r in range(cap)], axis=1)
+        lse = jnp.where(lane_s == row3, m + jnp.log(total), 0.0)
+        stats = [
+            jnp.sum(lse[n * block3:(n + 1) * block3], axis=0, keepdims=True)
+            for n in range(many)
+        ]
+        inverse = 1.0 / total
+        results = []
+        for n, own in enumerate(slot):
+            base = n * block3
+            values = jnp.concatenate([v_v[a] for a in own], axis=0)
+            o = (dot(w[base:base + block3], values) * inverse[base:base + block3]).astype(bf16)
+            both = [o[h * block:(h + 1) * block] for h in range(HEADS)]
+            results.append(jnp.concatenate(both, axis=1))
+        return results, stats
+
+    def serve_some(c, start, skip):
+        sources = [(me + 2 * ng - offset(start + n)) % ng for n in range(many)]
+        for src in sources[skip:]:
             remote(
                 recvq.at[c, src], recvq.at[c, src], q_send.at[c], q_recv.at[c, src],
                 {"group": src},
             ).wait_recv()
-            sendo[c, src] = cached(c, src)
+        results, stats = cached(c, sources)
+        if skip:
+            recvo[c, me] = results[0]
+            recvl[c, me] = stats[0]
+        for src, result, stat in zip(sources[skip:], results[skip:], stats[skip:]):
+            sendo[c, src] = result
+            sendl[c, src] = stat
+        for src in sources[skip:]:
             remote(
                 sendo.at[c, src], recvo.at[c, me], o_send.at[c], o_recv.at[c], {"group": src}
             ).start()
+            remote(
+                sendl.at[c, src], recvl.at[c, me], l_send.at[c], l_recv.at[c], {"group": src}
+            ).start()
+
+    def serve_span(c, lo, hi):
+        def go(i, carry):
+            serve_some(c, i * many, 0)
             return carry
 
-        lax.fori_loop(1, ng, go, 0)
+        if lo == 0:
+            serve_some(c, 0, 1)
+        lax.fori_loop(max(lo, 1), hi, go, 0)
+
+    batches = ng // many
+
+    def serve(c):
+        serve_span(c, 0, batches)
+
+    def serve_near(c):
+        serve_span(c, 0, batches // 2)
+
+    def serve_far(c):
+        serve_span(c, batches // 2, batches)
 
     def combine(c):
         span = pl.ds(0, ng - 1)
@@ -291,14 +413,26 @@
             sendo.at[c, span], recvo.at[c, span], o_send.at[c], o_recv.at[c],
             {"group": (me + 1) % ng},
         ).wait_recv()
-        pick = lax.broadcasted_iota(jnp.int32, (rows, slots), 1) == slot_col[...]
+        remote(
+            sendl.at[c, span], recvl.at[c, span], l_send.at[c], l_recv.at[c],
+            {"group": (me + 1) % ng},
+        ).wait_recv()
+        wide = jnp.concatenate([slot_col[...]] * (slots // 128), axis=1)
+        pick = count((rows, slots), 1) == wide
         pick = pick.astype(f32).astype(bf16)
-        back = dot(pick, recvo[c].reshape(slots, 512))
-        lane = lax.broadcasted_iota(jnp.int32, (rows, 128), 1) // 4
-        stat = back[:, 384:512]
+        back = dot(pick, recvo[c].reshape(slots, 384))
+        stat = recvl[c].reshape(ng, wide_l)
+        hi = stat.astype(bf16)
+        mid = (stat - hi.astype(f32)).astype(bf16)
+        lo = (stat - hi.astype(f32) - mid.astype(f32)).astype(bf16)
+        home = slot_col[:, 0:ng] // block
+        home = (count((rows, ng), 1) == home).astype(f32).astype(bf16)
+        terms = dot(home, jnp.concatenate([hi, mid, lo], axis=1))
+        stat = terms[:, 0:wide_l] + terms[:, wide_l:2 * wide_l] + terms[:, 2 * wide_l:]
+        spot = count((rows, wide_l), 1) - slot_col[:, 0:1] % block
         for h in range(HEADS):
             lanes = slice(h * 128, (h + 1) * 128)
-            cache_l = jnp.sum(jnp.where(lane == h, stat, 0.0), axis=1, keepdims=True)
+            cache_l = jnp.sum(jnp.where(spot == h * block, stat, 0.0), axis=1, keepdims=True)
             gap = newl[c, h] - cache_l
             a = 1.0 / (1.0 + jnp.exp(gap))
             b = 1.0 / (1.0 + jnp.exp(-gap))
@@ -355,44 +489,21 @@
         copy.start()
         outs.append(copy)
 
-    for c in range(chunks):
-        project(c)
-        route(c)
-        fresh(c)
-        if c == 0:
-            copies[3].wait()
-            copies[4].wait()
-        if c >= 1:
-            serve(c - 1)
-        if c >= 2:
-            combine(c - 2)
-            if c == 2:
-                for copy in wo_copies:
-                    copy.wait()
-            give(c - 2)
-            spread(c - 2)
-    last = chunks - 1
-    if chunks < 3:
-        for copy in wo_copies:
-            copy.wait()
-    serve(last)
-    if chunks >= 3:
-        relay(last - 2)
-    if chunks >= 2:
-        combine(last - 1)
-        give(last - 1)
-        spread(last - 1)
-    if chunks >= 3:
-        finish(last - 2)
-    if chunks >= 2:
-        relay(last - 1)
-    combine(last)
-    give(last)
-    spread(last)
-    if chunks >= 2:
-        finish(last - 1)
-    relay(last)
-    finish(last)
+    phases = {
+        "s": serve_near, "t": serve_far,
+        "A": project, "B": project_rest, "R": route, "F": fresh, "S": serve,
+        "C": combine, "V": give, "P": spread, "L": relay, "N": finish,
+    }
+    done = ""
+    for step in ORDER:
+        if step[0] in "Ss" and not set("Ss") & set(done):
+            for copy in copies + [table_copy]:
+                copy.wait()
+        if step[0] == "V" and "V" not in done:
+            for copy in wo_copies:
+                copy.wait()
+        phases[step[0]](int(step[1]))
+        done += step[0]
 
     for copy in pending:
         copy.wait_send()
@@ -406,6 +517,10 @@
             sendo.at[c, span], recvo.at[c, span], o_send.at[c], o_recv.at[c],
             {"group": (me + 1) % ng},
         ).wait_send()
+        remote(
+            sendl.at[c, span], recvl.at[c, span], l_send.at[c], l_recv.at[c],
+            {"group": (me + 1) % ng},
+        ).wait_send()
     for copy in outs:
         copy.wait()
 
@@ -415,6 +530,7 @@
     cs = steps // chunks
     rows = cs * part
     block = cap * cs
+    wide_l = -(-HEADS * block // 128) * 128
     any_ = pl.BlockSpec(memory_space=pl.ANY)
     vmem = pl.BlockSpec(memory_space=pltpu.VMEM)
     smem = pl.BlockSpec(memory_space=pltpu.SMEM)
@@ -424,26 +540,31 @@
         V((nt, steps, part, feat), bf16), V((nt, feat, 640), bf16), V((nt, 384, feat), bf16),
         V((part, 128, 128), bf16), V((part, 128, 128), bf16),
         V((steps * part, 128), f32), V((steps * part, 128), f32),
+        V((1, rows), jnp.int32), V((rows, 128), jnp.int32),
+        V((ng * part // 128, 128), jnp.int32),
+        pltpu.SMEM((ng * part // 128, 128), jnp.int32),
         V((rows, 640), f32), V((rows, 128), f32), V((chunks, rows, 384), bf16),
         V((steps * part, 128), bf16), V((steps * part, 128), bf16),
         V((chunks, rows, 384), f32), V((chunks, HEADS, rows, 128), f32),
         V((chunks, ng, block, 384), bf16), V((chunks, ng, block, 384), bf16),
-        V((chunks, ng, block, 512), bf16), V((chunks, ng, block, 512), bf16),
+        V((chunks, ng, block, 384), bf16), V((chunks, ng, block, 384), bf16),
+        V((chunks, ng, 1, wide_l), f32), V((chunks, ng, 1, wide_l), f32),
         V((rows, 384), bf16),
         V((chunks, 4, rows, feat), bf16), V((chunks, 4, rows, feat), bf16),
         V((chunks, 4, rows, feat), bf16),
         V((chunks, rows, feat), bf16), V((chunks, 2, rows // 2, feat), bf16),
         V((chunks, 2, 2, rows // 2, feat), bf16), V((chunks, 2, 2, rows // 2, feat), bf16),
         V((steps, part, feat), bf16),
-        dma((5 + 4 * nt,)), dma((chunks, 9)), dma((chunks, 9)),
+        dma((4 + 4 * nt,)), dma((chunks, 9)), dma((chunks, 9)),
         dma((chunks,)), dma((chunks, ng)), dma((chunks,)), dma((chunks,)),
+        dma((chunks,)), dma((chunks,)),
         dma((chunks, 4)), dma((chunks, 4)), dma((chunks, 2)), dma((chunks, 2)),
         dma((chunks, 2, 2)), dma((chunks, 2, 2)), dma((chunks,)),
     ]
     return pl.pallas_call(
         functools.partial(kernel, dims),
         out_shape=jax.ShapeDtypeStruct((steps, part, feat), bf16),
-        in_specs=[any_, vmem] + [any_] * 8 + [vmem, vmem, smem, smem],
+        in_specs=[any_, vmem] + [any_] * 6 + [vmem, vmem, vmem, smem, vmem],
         out_specs=any_,
         scratch_shapes=scratch,
         compiler_params=pltpu.CompilerParams(
@@ -460,42 +581,22 @@
     ng, nt = lax.axis_size("group"), lax.axis_size("tensor")
     cap = max(2, (2 * part + ng - 1) // ng)
     dims = (ng, nt, steps, part, feat, cap, CHUNKS)
-    cs = steps // CHUNKS
-    me = lax.axis_index("group")
-
-    sources = ancestor_group[:, 0].reshape(ng, part)
-    places = ancestor_slot.reshape(ng, part)
-    spans = lengths.reshape(ng, part)
-    asked = sources == me
-    rank = jnp.cumsum(asked.astype(jnp.int32), axis=1) - 1
-    chosen = asked[:, None, :] & (rank[:, None, :] == jnp.arange(cap)[None, :, None])
-    kidx = jnp.sum(jnp.where(chosen, places[:, None, :], 0), axis=2).reshape(-1)
-    my_lengths = lax.dynamic_index_in_dim(spans, me, 0, keepdims=False)
-    own_place = (kidx[:, None] == jnp.arange(part)[None, :])
-    kspan = jnp.sum(jnp.where(own_place, my_lengths[None, :], 0), axis=1)
-    mine = lax.dynamic_index_in_dim(sources, me, 0, keepdims=False)
-    my_place = lax.dynamic_index_in_dim(places, me, 0, keepdims=False)
-    earlier = jnp.arange(part)[None, :] < jnp.arange(part)[:, None]
-    my_rank = jnp.sum((mine[:, None] == mine[None, :]) & earlier, axis=1)
-    slot = mine * cap + my_rank
-    target = (slot[None, :] * cs + jnp.arange(cs, dtype=jnp.int32)[:, None]).reshape(-1)
-    my_span = jnp.take(lengths, mine * part + my_place)
-    position = (my_span[None, :] + jnp.arange(steps, dtype=jnp.int32)[:, None]).reshape(-1)
-    index = jnp.arange(64, dtype=f32)
-    inverse = THETA ** (-2.0 * index / 128)
-    angles = position.astype(f32)[:, None] * inverse
-    cos, sin = jnp.cos(angles), jnp.sin(angles)
-    cos = jnp.concatenate([cos, cos], axis=1)
-    sin = jnp.concatenate([-sin, sin], axis=1)
-
+    index = np.arange(64, dtype=np.float64)
+    inverse = np.float64(THETA) ** (-2.0 * index / 128)
+    wide = np.concatenate([inverse, inverse])
+    angles = np.arange(steps)[:, None] * wide[None, :]
+    turns = np.zeros((8 + 2 * steps, 128))
+    turns[0] = wide
+    turns[1] = np.where(np.arange(128) < 64, -1.0, 1.0)
+    turns[8:8 + steps] = np.cos(angles)
+    turns[8 + steps:] = np.sin(angles)
     out = call(
         dims,
         jnp.transpose(states, (1, 0, 2)),
         norm_gain.reshape(-1, 128),
         w_query, w_key, w_value, w_out, key_cache, value_cache,
-        cos, sin,
-        target[None, :], target[:, None],
-        kidx.astype(jnp.int32), kspan.astype(jnp.int32),
+        ancestor_group.reshape(-1, 128), ancestor_slot.reshape(-1, 128),
+        lengths.reshape(-1, 128), lengths, jnp.asarray(turns, f32),
     )
     return jnp.transpose(out, (1, 0, 2))
 

time: 148 us -> 109 us (0.74)
  Pallas kernels: 136 us -> 107 us
  other arithmetic: 5.2 us -> 0 us
  local copies, waits for them, and re-layouts: 6.86 us -> 2.23 us
    pallas_call x1, Pallas kernels: 136 us -> 107 us  [call(): pl.pallas_call(functools.partial(kernel, dims), out_shape=jax.ShapeDtypeS...]
where the time goes in v2:
time: 109 us
  Pallas kernels  107 us (98%)
  local copies, waits for them, and re-layouts  2.23 us (2%)
    pallas_call x1, Pallas kernels, call(): pl.pallas_call(functools.partial(kernel, dims), out_shape=jax.ShapeDtypeS...  107 us
    unnamed x1, local copies, waits for them, and re-layouts  2.23 us

profile of v2, /device:TPU:1, one launch (start us, length us, event | category | flops | bytes accessed | tf_op | source)
XLA Modules:
  0.0 109.1 jit_solution(10550782201460948051)
XLA Ops:
  0.0 106.9 %shard_map.118 = bf16[12,64,640]{2,1,0:T(8,128)(2,1)} custom-call(bf16[12,64,640]{2,1,0:T(8,128)(2,1)} %bitcast.7, f32[40,128]{1,0:T(8,128)} %bitcast.9, bf16[5120,384]{1,0:T(8,128)(2,1)} %wq_hbm.1, bf16[5120,128]{1,0:T(8,128)(2,1)} %wk_hbm.1, bf16[5120,128]{1,0:T(8,128)(2,1)} %wv_hbm.1, bf16[384,5120]{1,0:T(8,128)(2,1)} %wo_hbm.1, ...), custom_call_target="tpu_custom_call" | custom-call | tf_op jit(solution)/shard_map/pallas_call | solution.py:564
  106.9 2.2 %copy.14 = bf16[64,12,640]{2,0,1:T(8,128)(2,1)} copy(bf16[64,12,640]{2,0,1:T(8,128)(2,1)} %bitcast.6) | data formatting | bytes 1966080

commit v3 on v2

--- a/solution.py
+++ b/solution.py
@@ -233,9 +233,6 @@
     sl, sr, sf = shard_of(xl, core), shard_of(xr, core), shard_of(xf, core)
 
     def project(c):
-        shard_dot(t, c, True)
-        arrived(piece(partner, c), ag_recv.at[c, 2])
-        shard_dot(partner, c)
         arrived(piece(sl, c), ag_recv.at[c, 0])
         send(piece(sl, c, 0, hs), piece(sl, c, 0, hs), ag_send.at[c, 3], ag_recv.at[c, 3], right)
         send(piece(sl, c), piece(sl, c), ag_send.at[c, 4], ag_recv.at[c, 4], partner)
@@ -244,6 +241,9 @@
         send(piece(sr, c), piece(sr, c), ag_send.at[c, 6], ag_recv.at[c, 6], partner)
         if c + 1 < chunks:
             ag_start(c + 1)
+        shard_dot(t, c, True)
+        arrived(piece(partner, c), ag_recv.at[c, 2])
+        shard_dot(partner, c)
         shard_dot(sl, c)
         shard_dot(sr, c)
 

time: 109 us -> 109 us (level)
  no operation moved by 1% of the time
where the time goes in v3:
time: 109 us
  Pallas kernels  106 us (97%)
  local copies, waits for them, and re-layouts  2.23 us (2%)
    pallas_call x1, Pallas kernels, call(): pl.pallas_call(functools.partial(kernel, dims), out_shape=jax.ShapeDtypeS...  106 us
    unnamed x1, local copies, waits for them, and re-layouts  2.23 us

profile of v3, /device:TPU:1, one launch (start us, length us, event | category | flops | bytes accessed | tf_op | source)
XLA Modules:
  0.0 108.7 jit_solution(15509899963152164694)
XLA Ops:
  0.0 106.5 %shard_map.118 = bf16[12,64,640]{2,1,0:T(8,128)(2,1)} custom-call(bf16[12,64,640]{2,1,0:T(8,128)(2,1)} %bitcast.7, f32[40,128]{1,0:T(8,128)} %bitcast.9, bf16[5120,384]{1,0:T(8,128)(2,1)} %wq_hbm.1, bf16[5120,128]{1,0:T(8,128)(2,1)} %wk_hbm.1, bf16[5120,128]{1,0:T(8,128)(2,1)} %wv_hbm.1, bf16[384,5120]{1,0:T(8,128)(2,1)} %wo_hbm.1, ...), custom_call_target="tpu_custom_call" | custom-call | tf_op jit(solution)/shard_map/pallas_call | solution.py:564
  106.5 2.2 %copy.14 = bf16[64,12,640]{2,0,1:T(8,128)(2,1)} copy(bf16[64,12,640]{2,0,1:T(8,128)(2,1)} %bitcast.6) | data formatting | bytes 1966080
